TPU v7x, 512 devices: a whole 4x8x8 slice. The times are simulated.
512 devices in a mesh: role: 4 (over x), ep: 64 (over z, y), dp: 2 (over core).
Axes of the slice: x: 4, y: 8, z: 8, core: 2. Of those that a mesh axis runs over, the one named last changes fastest.
Arguments:
- latents: bfloat16 [16, 4096, 1536], P(('role', 'dp'), 'ep'), may hold values from -6 to 6
- noise: bfloat16 [1, 16, 4096, 1536], P(None, ('role', 'dp'), 'ep'), may hold values from -6 to 6
- expert_ids: int32 [1, 16, 4096, 6], P(None, ('role', 'dp'), 'ep'), may hold values from 0 to 63, all different within a row; in each aligned block of 64 rows (0 to 63, 64 to 127, ..., all dimensions but the last counted through in order) at most 7 rows name the same one
- gate_values: float32 [1, 16, 4096, 6], P(None, ('role', 'dp'), 'ep'), may hold values from 0.1 to 1
- advantages: float32 [16], P(('role', 'dp')), may hold values from -4 to 4
- expert_pair: bfloat16 [64, 2, 768, 1536], P('ep', None, ('role', 'dp')), may hold values from -6 to 6
Outputs:
- final_latents: bfloat16 [16, 4096, 1536], P(('role', 'dp'), 'ep')
- new_down: bfloat16 [64, 768, 1536], P('ep')
Inputs may be any that keep to these rules, and one draw needn't show every extreme that they name: `expert_ids`: each row names 6 different experts. In every aligned block of 64 rows (steps, images and tokens taken together in order; one index of ep holds one block of an image at a step) no expert is named more than 7 times, a bound that some block reaches.
All inputs are finite; a program needn't handle non-finite values.
Results may differ from a plain program's by a relative error of at most 0.008.
Values may be sent and summed in bfloat16 or wider, within the bound.
A program may use at most 128 MiB of HBM per device.

v0:
```python
import math
import jax
import jax.numpy as jnp
from jax import lax
from jax.sharding import PartitionSpec as P

CAP = 7


def coefficients(section):
    moment = 0.95 - 0.4 * section
    noise_level = 0.3 * math.sqrt(moment / (1.0 - moment))
    factor = noise_level * noise_level / (2.0 * moment)
    keep_gain = 1.0 - 0.4 * factor
    drift_gain = -0.4 * (1.0 + factor * (1.0 - moment))
    noise_gain = noise_level * math.sqrt(0.4)
    return (keep_gain, drift_gain, noise_gain)


def slot_matrices(picked, weights, experts, capacity):
    image_count, tokens, chosen_count = picked.shape
    flat_ids = picked.reshape(image_count, tokens * chosen_count)
    onehot = (flat_ids[..., None] == jnp.arange(experts, dtype=jnp.int32)).astype(jnp.int32)
    ranks = jnp.cumsum(onehot, axis=1) - 1
    placed = jnp.sum(ranks * onehot, axis=2)
    image_column = jnp.arange(image_count, dtype=jnp.int32)[:, None]
    slot_ids = (flat_ids * image_count + image_column) * capacity + placed
    slot_ids = slot_ids.reshape(image_count * tokens, chosen_count)
    total_slots = experts * image_count * capacity
    marked = (slot_ids[..., None] == jnp.arange(total_slots, dtype=jnp.int32)).astype(jnp.float32)
    selected = jnp.sum(marked, axis=1)
    flat_weights = weights.reshape(image_count * tokens, chosen_count)
    slot_gate = jnp.sum(jnp.sum(marked * flat_weights[..., None], axis=1), axis=0)
    return (slot_ids, selected, slot_gate, flat_weights)


def expert_pass(inputs, w_up, w_down):
    width = inputs.shape[-1]
    hidden_units = w_up.shape[1]
    pre_act = jnp.einsum("jlcd,lhd->jlch", inputs, w_up, preferred_element_type=jnp.float32) * (
        1.0 / math.sqrt(width)
    )
    hidden = jax.nn.gelu(pre_act, approximate=True).astype(jnp.bfloat16)
    output = jnp.einsum("jlch,lhd->jlcd", hidden, w_down, preferred_element_type=jnp.float32) * (
        1.0 / math.sqrt(hidden_units)
    )
    returned = lax.all_to_all(
        output.astype(jnp.bfloat16), "ep", split_axis=0, concat_axis=0, tiled=True
    )
    return (returned, hidden)


def per_device(latents, noise, expert_ids, gate_values, advantages, expert_pair):
    ep_size = lax.axis_size("ep")
    group_size = lax.axis_size("role") * lax.axis_size("dp")
    local_experts = expert_pair.shape[0]
    experts = local_experts * ep_size
    capacity = CAP
    image_count = latents.shape[0]
    tok_count = latents.shape[1]
    width = latents.shape[2]
    top_count = expert_ids.shape[3]
    total_slots = experts * image_count * capacity
    full_pair = lax.all_gather(expert_pair, ("role", "dp"), axis=2, tiled=True)
    w_up = full_pair[:, 0]
    w_down = full_pair[:, 1]
    hidden_units = full_pair.shape[2]
    current = latents.reshape(image_count * tok_count, width)
    image_of_slot = jnp.arange(total_slots, dtype=jnp.int32) // capacity % image_count
    keep_gain, drift_gain, noise_gain = coefficients(0)
    slot_ids, selected, slot_gate, flat_weights = slot_matrices(
        expert_ids[0], gate_values[0], experts, capacity
    )
    selected_half = selected.astype(jnp.bfloat16)
    noise_now = noise[0].reshape(image_count * tok_count, width)
    slot_latent = jnp.einsum(
        "ts,td->sd", selected_half, current, preferred_element_type=jnp.float32
    )
    slot_latent = slot_latent.astype(jnp.bfloat16).reshape(
        ep_size, local_experts, image_count * capacity, width
    )
    slot_noise = jnp.einsum(
        "ts,td->sd", selected_half, noise_now, preferred_element_type=jnp.float32
    )
    image_factor = advantages * (drift_gain / noise_gain)
    slot_scale = slot_gate * image_factor[image_of_slot]
    home_cot = (
        (slot_scale[:, None] * slot_noise)
        .astype(jnp.bfloat16)
        .reshape(ep_size, local_experts, image_count * capacity, width)
    )
    returned, hidden = expert_pass(
        lax.all_to_all(slot_latent, "ep", split_axis=0, concat_axis=0, tiled=True), w_up, w_down
    )
    returned, hidden, cotangent = (
        returned,
        hidden,
        lax.all_to_all(home_cot, "ep", split_axis=0, concat_axis=0, tiled=True),
    )
    back_rows = returned.reshape(total_slots, width)
    taken = jnp.take(back_rows, slot_ids, axis=0)
    velocity = jnp.sum(flat_weights[..., None] * taken.astype(jnp.float32), axis=1)
    moved = (
        keep_gain * current.astype(jnp.float32)
        + drift_gain * velocity
        + noise_gain * noise_now.astype(jnp.float32)
    )
    current = moved.astype(jnp.bfloat16)
    kept_hidden = [hidden]
    kept_cot = [cotangent]
    rate = 10.0 / math.sqrt(tok_count * ep_size * top_count * image_count * group_size / experts)
    total = jnp.zeros((hidden_units, local_experts, width), jnp.float32)
    for hidden, cotangent in zip(kept_hidden, kept_cot):
        total = jnp.einsum("jlch,jlcd->hld", hidden, cotangent, preferred_element_type=jnp.float32)
    summed = lax.psum(
        (total * (1.0 / math.sqrt(hidden_units)))
        .reshape(hidden_units, local_experts * width)
        .astype(jnp.bfloat16),
        ("role", "dp"),
    ).astype(jnp.float32)
    summed = jnp.transpose(summed.reshape(hidden_units, local_experts, width), (1, 0, 2))
    new_down = (w_down.astype(jnp.float32) + rate * summed).astype(jnp.bfloat16)
    return (current.reshape(image_count, tok_count, width), new_down)


def solution(mesh):
    in_specs = (
        P(("role", "dp"), "ep", None),
        P(None, ("role", "dp"), "ep", None),
        P(None, ("role", "dp"), "ep", None),
        P(None, ("role", "dp"), "ep", None),
        P(("role", "dp")),
        P("ep", None, ("role", "dp"), None),
    )
    out_specs = (P(("role", "dp"), "ep", None), P("ep", None, None))
    return jax.shard_map(
        per_device, mesh=mesh, in_specs=in_specs, out_specs=out_specs, check_vma=False
    )
```

profile of v0, /device:TPU:8, one launch (start us, length us, event | category | flops | bytes accessed | tf_op | source)
XLA Modules:
  0.0 347.8 jit_solution(13016884792895209371)
XLA Ops:
  7.2 0.8 copy.62
  8.2 0.7 broadcast_multiply_fusion.1
  9.0 1.8 reduce-window.6
  11.6 0.8 mul.176
  12.3 0.6 compare_and_fusion
  12.9 0.6 select_reduce_fusion
  13.5 1.9 convolution_convert_fusion
  15.4 2.5 reshape.262
  17.9 16.9 %all-to-all-start = ((bf16[64,1,14,1536]{3,2,1,0:T(8,128)(2,1)}), bf16[64,1,14,1536]{3,2,1,0:T(8,128)(2,1)}, u32[]{:S(2)}, u32[]{:S(2)}) async-start(bf16[64,1,14,1536]{3,2,1,0:T(8,128)(2,1)} %bitcast.3), calls=%async_computation | async-start | bytes 6291456 | tf_op jit(solution)/shard_map/all_to_all | solution.py:93
  34.9 0.7 all-gather.2.cloned.1.call-update
  35.6 0.6 fusion.34
  36.2 1.3 fusion.30
  37.5 0.9 multiply_convert_fusion
  38.4 2.6 reshape.268
  41.0 73.6 %all-to-all-done = bf16[64,1,14,1536]{3,2,1,0:T(8,128)(2,1)} async-done(((bf16[64,1,14,1536]{3,2,1,0:T(8,128)(2,1)}), bf16[64,1,14,1536]{3,2,1,0:T(8,128)(2,1)}, u32[]{:S(2)}, u32[]{:S(2)}) %all-to-all-start) | async-done | bytes 2752544 | tf_op jit(solution)/shard_map/all_to_all | solution.py:93
  114.6 22.3 %all-to-all-start.2 = ((bf16[64,1,14,1536]{3,2,1,0:T(8,128)(2,1)}), bf16[64,1,14,1536]{3,2,1,0:T(8,128)(2,1)S(1)}, u32[]{:S(2)}, u32[]{:S(2)}) async-start(bf16[64,1,14,1536]{3,2,1,0:T(8,128)(2,1)} %bitcast.23), calls=%async_computation.2 | async-start | bytes 6291456 | tf_op jit(solution)/shard_map/all_to_all | solution.py:98
  136.9 8.1 %fusion.21 = bf16[64,14,768]{2,0,1:T(8,128)(2,1)S(1)} fusion(bf16[1,2,768,1536]{3,2,1,0:T(8,128)(2,1)} %all-gather.2.cloned.1.call-done, bf16[64,1,14,1536]{3,2,1,0:T(8,128)(2,1)} %all-to-all-done), kind=kOutput, calls=%fused_computation.31 | convolution fusion | flops 2120810496 | bytes 6881280 | tf_op jit(solution)/shard_map/jlcd,lhd->jlch/dot_general | solution.py:40
  145.0 2.3 fusion.1
  147.3 3.2 copy.71
  150.5 62.1 %all-to-all-done.2 = bf16[64,1,14,1536]{3,2,1,0:T(8,128)(2,1)S(1)} async-done(((bf16[64,1,14,1536]{3,2,1,0:T(8,128)(2,1)}), bf16[64,1,14,1536]{3,2,1,0:T(8,128)(2,1)S(1)}, u32[]{:S(2)}, u32[]{:S(2)}) %all-to-all-start.2) | async-done | bytes 2752544 | tf_op jit(solution)/shard_map/all_to_all | solution.py:98
  212.6 21.0 %all-to-all-start.1 = ((bf16[64,1,14,1536]{3,2,1,0:T(8,128)(2,1)}), bf16[64,1,14,1536]{3,2,1,0:T(8,128)(2,1)}, u32[]{:S(2)}, u32[]{:S(2)}) async-start(bf16[64,1,14,1536]{3,2,1,0:T(8,128)(2,1)} %copy.71), calls=%async_computation.1 | async-start | bytes 6291456 | tf_op jit(solution)/shard_map/all_to_all | solution.py:47
  233.9 7.0 %fusion.2 = bf16[768,1536]{1,0:T(8,128)(2,1)} fusion(bf16[64,14,768]{2,0,1:T(8,128)(2,1)} %copy-done.5, bf16[64,1,14,1536]{3,2,1,0:T(8,128)(2,1)S(1)} %all-to-all-done.2), kind=kOutput, calls=%fused_computation.10 | convolution fusion | flops 2116288512 | bytes 6488064 | tf_op jit(solution)/shard_map/jlch,jlcd->hld/dot_general | solution.py:114
  241.2 0.7 copy.61
  242.0 0.7 compare_select_fusion.1
  242.9 0.8 copy.68
  243.7 76.6 %all-reduce.2.cloned.1.call-done = bf16[768,1536]{1,0:T(8,128)(2,1)} async-done(((bf16[768,1536]{1,0:T(8,128)(2,1)}), bf16[768,1536]{1,0:T(8,128)(2,1)}) %all-reduce.2.cloned.1.call-update) | async-done | bytes 2359312 | tf_op jit(solution)/shard_map/psum | solution.py:115
  320.3 4.5 %fusion.16 = bf16[1,768,1536]{2,1,0:T(8,128)(2,1)} fusion(bf16[768,1536]{1,0:T(8,128)(2,1)} %all-reduce.2.cloned.1.call-done, bf16[1,2,768,1536]{3,2,1,0:T(8,128)(2,1)} %all-gather.2.cloned.1.call-done), kind=kLoop, calls=%fused_computation.27 | loop fusion | flops 5898240 | bytes 7077888 | tf_op jit(solution)/shard_map/convert_element_type | solution.py:122
  324.8 3.8 %reshape.267 = bf16[896,1536]{1,0:T(8,128)(2,1)S(1)} reshape(bf16[64,1,14,1536]{3,2,1,0:T(8,128)(2,1)} %all-to-all-done.1) | data formatting | bytes 5505024 | tf_op jit(solution)/shard_map/reshape | solution.py:100
  328.6 3.8 %gather_fusion = bf16[768,1536]{1,0:T(8,128)(2,1)} fusion(bf16[896,1536]{1,0:T(8,128)(2,1)S(1)} %reshape.267, s32[1024]{0:T(1024)S(1)} %pad_clamp_fusion), kind=kCustom, calls=%fused_computation | custom fusion | bytes 4721664 | tf_op jit(solution)/shard_map/jit(_take)/gather | solution.py:101
  332.4 3.5 %reshape.271 = bf16[128,6,1536]{2,1,0:T(8,128)(2,1)S(1)} reshape(bf16[768,1536]{1,0:T(8,128)(2,1)} %gather_fusion) | data formatting | bytes 4718592 | tf_op jit(solution)/shard_map/jit(_take)/gather | solution.py:101
  336.0 4.0 %multiply_reduce_fusion = f32[128,1536]{1,0:T(8,128)S(1)} fusion(bf16[128,6,1536]{2,1,0:T(8,128)(2,1)S(1)} %reshape.271, f32[128,6]{1,0:T(8,128)} %copy.61, pred[128,6]{1,0:T(8,128)(4,1)S(1)} %copy.68), kind=kLoop, calls=%fused_computation.1 | loop fusion | flops 4521984 | bytes 3149568 | tf_op jit(solution)/shard_map/reduce_sum | solution.py:102
  340.1 0.9 fusion.24
  (40 shorter events, 2.0 us)
Async XLA Ops:
  11.6 6.4 %copy-start.3 = (s32[128]{0:T(128)}, s32[128]{0:T(128)S(1)}, u32[]{:S(2)}) copy-start(s32[128]{0:T(128)S(1)} %add.131) | copy-start | bytes 1540
  17.9 17.6 %copy-start.4 = (f32[2]{0:T(128)S(1)}, f32[2]{0:T(128)}, u32[]{:S(2)}) copy-start(f32[2]{0:T(128)} %param.10) | copy-start | bytes 28
  17.9 19.6 %copy-start = (bf16[1,2,64,1536]{3,2,1,0:T(8,128)(2,1)S(1)}, bf16[1,2,64,1536]{3,2,1,0:T(8,128)(2,1)}, u32[]{:S(2)}) copy-start(bf16[1,2,64,1536]{3,2,1,0:T(8,128)(2,1)} %param.7) | copy-start | bytes 1179652
  17.9 96.6 %all-to-all-start = ((bf16[64,1,14,1536]{3,2,1,0:T(8,128)(2,1)}), bf16[64,1,14,1536]{3,2,1,0:T(8,128)(2,1)}, u32[]{:S(2)}, u32[]{:S(2)}) async-start(bf16[64,1,14,1536]{3,2,1,0:T(8,128)(2,1)} %bitcast.3), calls=%async_computation | async-start | bytes 6291456 | tf_op jit(solution)/shard_map/all_to_all | solution.py:93
  34.8 102.1 %all-gather.2.cloned.1.call-start = ((), (), s32[]{:S(2)}) async-start(), calls=%async_computation.3 | async-start | bytes 5308416 | tf_op jit(solution)/shard_map/all_gather | solution.py:64
  114.6 98.0 %all-to-all-start.2 = ((bf16[64,1,14,1536]{3,2,1,0:T(8,128)(2,1)}), bf16[64,1,14,1536]{3,2,1,0:T(8,128)(2,1)S(1)}, u32[]{:S(2)}, u32[]{:S(2)}) async-start(bf16[64,1,14,1536]{3,2,1,0:T(8,128)(2,1)} %bitcast.23), calls=%async_computation.2 | async-start | bytes 6291456 | tf_op jit(solution)/shard_map/all_to_all | solution.py:98
  136.9 8.1 %copy-start.2 = (bf16[1,2,768,1536]{3,2,1,0:T(8,128)(2,1)S(1)}, bf16[1,2,768,1536]{3,2,1,0:T(8,128)(2,1)}, u32[]{:S(2)}) copy-start(bf16[1,2,768,1536]{3,2,1,0:T(8,128)(2,1)} %all-gather.2.cloned.1.call-done) | copy-start | bytes 14155780
  145.0 2.3 copy-start.5
  212.6 112.2 %all-to-all-start.1 = ((bf16[64,1,14,1536]{3,2,1,0:T(8,128)(2,1)}), bf16[64,1,14,1536]{3,2,1,0:T(8,128)(2,1)}, u32[]{:S(2)}, u32[]{:S(2)}) async-start(bf16[64,1,14,1536]{3,2,1,0:T(8,128)(2,1)} %copy.71), calls=%async_computation.1 | async-start | bytes 6291456 | tf_op jit(solution)/shard_map/all_to_all | solution.py:47
  233.6 86.7 %all-reduce.2.cloned.1.call-start = ((), (), s32[]{:S(2)}) async-start(), calls=%async_computation.4 | async-start | bytes 4718592 | tf_op jit(solution)/shard_map/psum | solution.py:115
  336.0 4.1 %copy-start.1 = (bf16[2,64,1536]{2,1,0:T(8,128)(2,1)S(1)}, bf16[2,64,1536]{2,1,0:T(8,128)(2,1)}, u32[]{:S(2)}) copy-start(bf16[2,64,1536]{2,1,0:T(8,128)(2,1)} %param.6) | copy-start | bytes 1179652
Sparse Core Ops, SparseCore 0:
  37.8 40.3 all-gather.1
  241.1 79.2 all-reduce.1
where the time goes:
time: 349 us; the launch traced here: 348 us
  waiting for transfers between devices  213 us (61%)
  starting transfers between devices  60.5 us (17%)
  local copies, waits for them, and re-layouts  24.5 us (7%)
  matrix products  20.2 us (6%)
  other arithmetic  15.4 us (4%)
  between operations  14.3 us (4%)
    psum x1, waiting for transfers between devices, per_device(): lax.psum((total * (1.0 / math.sqrt(hidden_units))).reshape(hidden_units,...  76.6 us
    all_to_all x1, waiting for transfers between devices, per_device(): lax.all_to_all(slot_latent, 'ep', split_axis=0, concat_axis=0, tiled=True)  73.6 us
    all_to_all x1, waiting for transfers between devices, per_device(): lax.all_to_all(home_cot, 'ep', split_axis=0, concat_axis=0, tiled=True)  62.1 us
    all_to_all x1, starting transfers between devices, per_device(): lax.all_to_all(home_cot, 'ep', split_axis=0, concat_axis=0, tiled=True)  22.3 us
    all_to_all x1, starting transfers between devices, expert_pass(): lax.all_to_all(output.astype(jnp.bfloat16), 'ep', split_axis=0, concat_ax...  21 us
    all_to_all x1, starting transfers between devices, per_device(): lax.all_to_all(slot_latent, 'ep', split_axis=0, concat_axis=0, tiled=True)  16.9 us
    dot_general x1, matrix products, expert_pass(): jnp.einsum('jlcd,lhd->jlch', inputs, w_up, preferred_element_type=jnp.flo...  8.06 us
    gather x2, local copies, waits for them, and re-layouts, per_device(): taken = jnp.take(back_rows, slot_ids, axis=0)  7.35 us
  transfers between devices with their start and end apart: 5, of which 3 were waited for; matrix products, arithmetic and copies ran while one was open for 10% of the time, Pallas kernels for 0%

commit v1 on v0

--- a/solution.py
+++ b/solution.py
@@ -51,6 +51,12 @@
 
 
 def per_device(latents, noise, expert_ids, gate_values, advantages, expert_pair):
+
+    def convert_scales(vector, axis_id, mesh_dim="dp"):
+        even = lax.psum(vector, axis_id)
+        tall = lax.psum(even, mesh_dim)
+        return tall
+
     ep_size = lax.axis_size("ep")
     group_size = lax.axis_size("role") * lax.axis_size("dp")
     local_experts = expert_pair.shape[0]
@@ -112,11 +118,11 @@
     total = jnp.zeros((hidden_units, local_experts, width), jnp.float32)
     for hidden, cotangent in zip(kept_hidden, kept_cot):
         total = jnp.einsum("jlch,jlcd->hld", hidden, cotangent, preferred_element_type=jnp.float32)
-    summed = lax.psum(
+    summed = convert_scales(
         (total * (1.0 / math.sqrt(hidden_units)))
         .reshape(hidden_units, local_experts * width)
         .astype(jnp.bfloat16),
-        ("role", "dp"),
+        "role",
     ).astype(jnp.float32)
     summed = jnp.transpose(summed.reshape(hidden_units, local_experts, width), (1, 0, 2))
     new_down = (w_down.astype(jnp.float32) + rate * summed).astype(jnp.bfloat16)

time: 349 us -> 386 us (1.11)
  the two profiles are of different devices: /device:TPU:8 before, /device:TPU:1 now
where the time goes in v1:
time: 386 us
  waiting for transfers between devices  246 us (64%)
  starting transfers between devices  66.5 us (17%)
  local copies, waits for them, and re-layouts  23.9 us (6%)
  matrix products  20.2 us (5%)
  other arithmetic  14.7 us (4%)
  between operations  14 us (4%)
    psum x1, waiting for transfers between devices, convert_scales(): even = lax.psum(vector, axis_id)  76 us
    all_to_all x1, waiting for transfers between devices, per_device(): lax.all_to_all(slot_latent, 'ep', split_axis=0, concat_axis=0, tiled=True)  67 us
    all_to_all x1, waiting for transfers between devices, per_device(): lax.all_to_all(home_cot, 'ep', split_axis=0, concat_axis=0, tiled=True)  61.7 us
    psum x1, waiting for transfers between devices, convert_scales(): tall = lax.psum(even, mesh_dim)  40.8 us
    all_to_all x1, starting transfers between devices, per_device(): lax.all_to_all(home_cot, 'ep', split_axis=0, concat_axis=0, tiled=True)  27.8 us
    all_to_all x1, starting transfers between devices, expert_pass(): lax.all_to_all(output.astype(jnp.bfloat16), 'ep', split_axis=0, concat_ax...  20.9 us
    all_to_all x1, starting transfers between devices, per_device(): lax.all_to_all(slot_latent, 'ep', split_axis=0, concat_axis=0, tiled=True)  17.5 us
    dot_general x1, matrix products, expert_pass(): jnp.einsum('jlcd,lhd->jlch', inputs, w_up, preferred_element_type=jnp.flo...  8.06 us
  transfers between devices with their start and end apart: 6, of which 4 were waited for; matrix products, arithmetic and copies ran while one was open for 8% of the time, Pallas kernels for 0%

profile of v1, /device:TPU:1, one launch (start us, length us, event | category | flops | bytes accessed | tf_op | source)
XLA Modules:
  0.0 385.5 jit_solution(12458772846229841662)
XLA Ops:
  7.2 0.8 copy.62
  8.2 0.7 broadcast_multiply_fusion.1
  9.0 1.8 reduce-window.6
  11.6 0.8 mul.176
  12.3 0.5 compare_and_fusion
  12.9 0.6 select_reduce_fusion
  13.5 1.9 convolution_convert_fusion
  15.4 2.5 reshape.262
  17.9 17.5 %all-to-all-start = ((bf16[64,1,14,1536]{3,2,1,0:T(8,128)(2,1)}), bf16[64,1,14,1536]{3,2,1,0:T(8,128)(2,1)}, u32[]{:S(2)}, u32[]{:S(2)}) async-start(bf16[64,1,14,1536]{3,2,1,0:T(8,128)(2,1)} %bitcast.3), calls=%async_computation | async-start | bytes 6291456 | tf_op jit(solution)/shard_map/all_to_all | solution.py:99
  35.4 0.7 all-gather.2.cloned.1.call-update
  36.2 0.6 fusion.34
  36.7 1.3 fusion.30
  38.1 0.9 multiply_convert_fusion
  39.0 2.6 reshape.268
  41.6 67.0 %all-to-all-done = bf16[64,1,14,1536]{3,2,1,0:T(8,128)(2,1)} async-done(((bf16[64,1,14,1536]{3,2,1,0:T(8,128)(2,1)}), bf16[64,1,14,1536]{3,2,1,0:T(8,128)(2,1)}, u32[]{:S(2)}, u32[]{:S(2)}) %all-to-all-start) | async-done | bytes 2752544 | tf_op jit(solution)/shard_map/all_to_all | solution.py:99
  108.6 27.8 %all-to-all-start.2 = ((bf16[64,1,14,1536]{3,2,1,0:T(8,128)(2,1)}), bf16[64,1,14,1536]{3,2,1,0:T(8,128)(2,1)S(1)}, u32[]{:S(2)}, u32[]{:S(2)}) async-start(bf16[64,1,14,1536]{3,2,1,0:T(8,128)(2,1)} %bitcast.23), calls=%async_computation.2 | async-start | bytes 6291456 | tf_op jit(solution)/shard_map/all_to_all | solution.py:104
  136.5 8.1 %fusion.21 = bf16[64,14,768]{2,0,1:T(8,128)(2,1)S(1)} fusion(bf16[1,2,768,1536]{3,2,1,0:T(8,128)(2,1)} %all-gather.2.cloned.1.call-done, bf16[64,1,14,1536]{3,2,1,0:T(8,128)(2,1)} %all-to-all-done), kind=kOutput, calls=%fused_computation.31 | convolution fusion | flops 2120810496 | bytes 6881280 | tf_op jit(solution)/shard_map/jlcd,lhd->jlch/dot_general | solution.py:40
  144.5 2.3 fusion.1
  146.8 3.2 copy.71
  150.0 61.7 %all-to-all-done.2 = bf16[64,1,14,1536]{3,2,1,0:T(8,128)(2,1)S(1)} async-done(((bf16[64,1,14,1536]{3,2,1,0:T(8,128)(2,1)}), bf16[64,1,14,1536]{3,2,1,0:T(8,128)(2,1)S(1)}, u32[]{:S(2)}, u32[]{:S(2)}) %all-to-all-start.2) | async-done | bytes 2752544 | tf_op jit(solution)/shard_map/all_to_all | solution.py:104
  211.7 20.9 %all-to-all-start.1 = ((bf16[64,1,14,1536]{3,2,1,0:T(8,128)(2,1)}), bf16[64,1,14,1536]{3,2,1,0:T(8,128)(2,1)}, u32[]{:S(2)}, u32[]{:S(2)}) async-start(bf16[64,1,14,1536]{3,2,1,0:T(8,128)(2,1)} %copy.71), calls=%async_computation.1 | async-start | bytes 6291456 | tf_op jit(solution)/shard_map/all_to_all | solution.py:47
  232.7 7.0 %fusion.2 = bf16[768,1536]{1,0:T(8,128)(2,1)} fusion(bf16[64,14,768]{2,0,1:T(8,128)(2,1)} %copy-done.7, bf16[64,1,14,1536]{3,2,1,0:T(8,128)(2,1)S(1)} %all-to-all-done.2), kind=kOutput, calls=%fused_computation.10 | convolution fusion | flops 2116288512 | bytes 6488064 | tf_op jit(solution)/shard_map/jlch,jlcd->hld/dot_general | solution.py:120
  239.7 0.3 all-reduce.5.cloned.1.call-start
  240.0 76.0 %all-reduce.3.cloned.1.call-done = bf16[768,1536]{1,0:T(8,128)(2,1)} async-done(((bf16[768,1536]{1,0:T(8,128)(2,1)}), bf16[768,1536]{1,0:T(8,128)(2,1)}) %all-reduce.3.cloned.1.call-update) | async-done | bytes 2359312 | tf_op jit(solution)/shard_map/psum | solution.py:56
  316.3 0.7 copy.61
  317.5 40.8 %all-reduce.5.cloned.1.call-done = bf16[768,1536]{1,0:T(8,128)(2,1)} async-done(((bf16[768,1536]{1,0:T(8,128)(2,1)}), bf16[768,1536]{1,0:T(8,128)(2,1)}) %all-reduce.5.cloned.1.call-update) | async-done | bytes 2359312 | tf_op jit(solution)/shard_map/psum | solution.py:57
  358.3 4.5 %fusion.16 = bf16[1,768,1536]{2,1,0:T(8,128)(2,1)} fusion(bf16[768,1536]{1,0:T(8,128)(2,1)} %all-reduce.5.cloned.1.call-done, bf16[1,2,768,1536]{3,2,1,0:T(8,128)(2,1)} %all-gather.2.cloned.1.call-done), kind=kLoop, calls=%fused_computation.27 | loop fusion | flops 5898240 | bytes 7077888 | tf_op jit(solution)/shard_map/convert_element_type | solution.py:128
  362.8 3.8 reshape.267
  366.6 3.8 gather_fusion
  370.4 3.5 reshape.271
  374.0 4.0 %multiply_reduce_fusion = f32[128,1536]{1,0:T(8,128)S(1)} fusion(bf16[128,6,1536]{2,1,0:T(8,128)(2,1)S(1)} %reshape.271, f32[128,6]{1,0:T(8,128)} %copy.61, pred[128,6]{1,0:T(8,128)(4,1)S(1)} %copy.68), kind=kLoop, calls=%fused_computation.1 | loop fusion | flops 4521984 | bytes 3149568 | tf_op jit(solution)/shard_map/reduce_sum | solution.py:108
  378.1 0.9 fusion.24
  (47 shorter events, 2.0 us)
Async XLA Ops:
  11.6 6.3 %copy-start.4 = (s32[128]{0:T(128)}, s32[128]{0:T(128)S(1)}, u32[]{:S(2)}) copy-start(s32[128]{0:T(128)S(1)} %add.133) | copy-start | bytes 1540
  17.9 18.3 %copy-start.6 = (f32[2]{0:T(128)S(1)}, f32[2]{0:T(128)}, u32[]{:S(2)}) copy-start(f32[2]{0:T(128)} %param.10) | copy-start | bytes 28
  17.9 20.2 %copy-start = (bf16[1,2,64,1536]{3,2,1,0:T(8,128)(2,1)S(1)}, bf16[1,2,64,1536]{3,2,1,0:T(8,128)(2,1)}, u32[]{:S(2)}) copy-start(bf16[1,2,64,1536]{3,2,1,0:T(8,128)(2,1)} %param.7) | copy-start | bytes 1179652
  17.9 90.7 %all-to-all-start = ((bf16[64,1,14,1536]{3,2,1,0:T(8,128)(2,1)}), bf16[64,1,14,1536]{3,2,1,0:T(8,128)(2,1)}, u32[]{:S(2)}, u32[]{:S(2)}) async-start(bf16[64,1,14,1536]{3,2,1,0:T(8,128)(2,1)} %bitcast.3), calls=%async_computation | async-start | bytes 6291456 | tf_op jit(solution)/shard_map/all_to_all | solution.py:99
  35.4 101.0 %all-gather.2.cloned.1.call-start = ((), (), s32[]{:S(2)}) async-start(), calls=%async_computation.3 | async-start | bytes 5308416 | tf_op jit(solution)/shard_map/all_gather | solution.py:70
  108.6 103.1 %all-to-all-start.2 = ((bf16[64,1,14,1536]{3,2,1,0:T(8,128)(2,1)}), bf16[64,1,14,1536]{3,2,1,0:T(8,128)(2,1)S(1)}, u32[]{:S(2)}, u32[]{:S(2)}) async-start(bf16[64,1,14,1536]{3,2,1,0:T(8,128)(2,1)} %bitcast.23), calls=%async_computation.2 | async-start | bytes 6291456 | tf_op jit(solution)/shard_map/all_to_all | solution.py:104
  136.4 8.1 %copy-start.2 = (bf16[1,2,768,1536]{3,2,1,0:T(8,128)(2,1)S(1)}, bf16[1,2,768,1536]{3,2,1,0:T(8,128)(2,1)}, u32[]{:S(2)}) copy-start(bf16[1,2,768,1536]{3,2,1,0:T(8,128)(2,1)} %all-gather.2.cloned.1.call-done) | copy-start | bytes 14155780
  144.5 2.3 copy-start.7
  211.7 151.1 %all-to-all-start.1 = ((bf16[64,1,14,1536]{3,2,1,0:T(8,128)(2,1)}), bf16[64,1,14,1536]{3,2,1,0:T(8,128)(2,1)}, u32[]{:S(2)}, u32[]{:S(2)}) async-start(bf16[64,1,14,1536]{3,2,1,0:T(8,128)(2,1)} %copy.71), calls=%async_computation.1 | async-start | bytes 6291456 | tf_op jit(solution)/shard_map/all_to_all | solution.py:47
  232.6 83.4 %all-reduce.3.cloned.1.call-start = ((), (), s32[]{:S(2)}) async-start(), calls=%async_computation.4 | async-start | bytes 4718592 | tf_op jit(solution)/shard_map/psum | solution.py:56
  239.7 77.4 %copy-start.5 = (s32[128]{0:T(128)S(1)}, s32[128]{0:T(128)}, u32[]{:S(2)}) copy-start(s32[128]{0:T(128)} %copy-done.4) | copy-start | bytes 1540
  239.7 77.7 %copy-start.3 = (pred[128,6]{0,1:T(8,128)(4,1)S(1)}, pred[128,6]{0,1:T(8,128)(4,1)}, u32[]{:S(2)}) copy-start(pred[128,6]{0,1:T(8,128)(4,1)} %get-tuple-element.4) | copy-start | bytes 2308
  239.7 118.6 %all-reduce.5.cloned.1.call-start = ((), (), s32[]{:S(2)}) async-start(), calls=%async_computation.5 | async-start | bytes 4718592 | tf_op jit(solution)/shard_map/psum | solution.py:57
  374.0 4.1 %copy-start.1 = (bf16[2,64,1536]{2,1,0:T(8,128)(2,1)S(1)}, bf16[2,64,1536]{2,1,0:T(8,128)(2,1)}, u32[]{:S(2)}) copy-start(bf16[2,64,1536]{2,1,0:T(8,128)(2,1)} %param.6) | copy-start | bytes 1179652
Sparse Core Ops, SparseCore 0:
  38.4 41.0 all-gather.1
  239.8 76.1 all-reduce.2
  318.9 39.3 all-reduce.4
